TPU v7x, 256 devices: a whole 4x4x8 slice. The times are simulated.
256 devices in a mesh: lat: 8 (over x, y_lo), lon: 32 (over y_hi, z, core).
Axes of the slice: x: 4, y: 4 (y_hi: 2, y_lo: 2; y = y_hi * 2 + y_lo), z: 8, core: 2. Of those that a mesh axis runs over, the one named last changes fastest.
Arguments:
- forcing: float32 [2, 2, 8, 128, 256], P(None, None, None, 'lat', 'lon'), may hold values from -6 to 6
- zonal: float32 [8, 128, 256], P(None, 'lat', 'lon'), may hold values from -0.3 to 0.3
- meridional: float32 [8, 128, 256], P(None, 'lat', 'lon'), may hold values from -0.3 to 0.3
- mixing: float32 [7, 128, 256], P(None, 'lat', 'lon'), may hold values from 0.03 to 0.24
- panel: bfloat16 [32768, 8, 4096], P('lat', None, 'lon'), may hold values from -0.046875 to 0.046875
Outputs:
- adjoint_state: float32 [2, 8, 128, 256], P(None, None, 'lat', 'lon')
- state_grad: float32 [2, 8, 8, 4096], P(None, None, 'lat', 'lon')
- flux_grad: float32 [2, 8, 4096], P(None, 'lat', 'lon')
All inputs are finite; a program needn't handle non-finite values.
Results may differ from a plain program's by a relative error of at most 0.0029.
Values may be sent and summed in bfloat16 or wider, within the bound.
A program may use at most 64 MiB of HBM per device.

v0:
```python
import jax
import jax.numpy as jnp
from jax import lax
from jax.sharding import PartitionSpec as P


def extended(value, sides, width, wrap):
    for axis, dim in sides:
        peers, length = (lax.axis_size(axis), value.shape[dim])
        up = [(i, (i + 1) % peers) for i in range(peers if wrap else peers - 1)]
        down = [(j, i) for i, j in up]
        last = lax.slice_in_dim(value, length - width, length, axis=dim)
        initial = lax.slice_in_dim(value, 0, width, axis=dim)
        before = lax.ppermute(last, axis, up)
        after = lax.ppermute(initial, axis, down)
        value = jnp.concatenate([before, value, after], axis=dim)
    return value


def diffuse(tracer, mixing):
    flow = mixing * (tracer[..., 1:, :, :] - tracer[..., :-1, :, :])
    zeros = jnp.zeros_like(flow[..., :1, :, :])
    return tracer + jnp.concatenate([flow, zeros], -3) - jnp.concatenate([zeros, flow], -3)


def advect_local(tracer, zonal_ext, merid_ext):
    centre = tracer[..., 1:-1, 1:-1]
    out_east = jnp.maximum(zonal_ext[:, 1:-1, 1:-1], 0.0)
    in_west = jnp.minimum(zonal_ext[:, 1:-1, :-2], 0.0)
    out_north = jnp.maximum(merid_ext[:, 1:-1, 1:-1], 0.0)
    in_south = jnp.minimum(merid_ext[:, :-2, 1:-1], 0.0)
    return (
        centre * (1.0 - out_east + in_west - out_north + in_south)
        + tracer[..., 1:-1, 2:] * out_east
        - tracer[..., 1:-1, :-2] * in_west
        + tracer[..., 2:, 1:-1] * out_north
        - tracer[..., :-2, 1:-1] * in_south
    )


def widen(planes):
    widened = extended(planes, (("lon", 2),), 1, True)
    return extended(widened, (("lat", 1),), 1, False)


def row_adder(panel, piece):
    return jnp.einsum("rc,cam->ram", piece, panel, preferred_element_type=jnp.float32)


def precondition(vectors, panel):
    total = row_adder(panel, lax.all_gather(vectors, "lon", axis=1, tiled=True))
    return lax.psum_scatter(total, "lat", scatter_dimension=1, tiled=True)


def shards(forcing, zonal, meridional, mixing, panel):
    levels, band_rows, band_cols = zonal.shape
    cell_count = band_rows * band_cols
    row_index = lax.axis_index("lat") * band_rows + jnp.arange(band_rows, dtype=jnp.int32)
    total_rows = band_rows * lax.axis_size("lat")
    top_mask = (row_index < total_rows - 1).astype(jnp.float32)[None, :, None]
    merid_masked = meridional * top_mask
    started = diffuse(forcing[1], mixing).reshape(2 * levels, band_rows, band_cols)
    widened = widen(jnp.concatenate([started, zonal, merid_masked], 0))
    costate_ext = widened[: 2 * levels].reshape(2, levels, band_rows + 2, band_cols + 2)
    zonal_ext = widened[2 * levels : 3 * levels]
    merid_ext = widened[3 * levels :]
    middle = advect_local(costate_ext, zonal_ext, merid_ext) + forcing[0]
    surface = forcing[1][:, 0] + middle[:, 0]
    flux_vec = surface.reshape(2, cell_count).astype(jnp.bfloat16)
    mixed = diffuse(middle, mixing).reshape(2 * levels, band_rows, band_cols)
    mixed_ext = widen(mixed).reshape(2, levels, band_rows + 2, band_cols + 2)
    adjoint_state = advect_local(mixed_ext, zonal_ext, merid_ext)
    state_vec = adjoint_state.reshape(2 * levels, cell_count).astype(jnp.bfloat16)
    summed = precondition(jnp.concatenate([flux_vec, state_vec], 0), panel)
    flux_grad = summed[:2]
    state_grad = summed[2:].reshape(2, levels, summed.shape[1], summed.shape[2])
    return (adjoint_state, state_grad, flux_grad)


def solution(mesh):
    return jax.shard_map(
        shards,
        mesh=mesh,
        in_specs=(
            P(None, None, None, "lat", "lon"),
            P(None, "lat", "lon"),
            P(None, "lat", "lon"),
            P(None, "lat", "lon"),
            P("lat", None, "lon"),
        ),
        out_specs=(P(None, None, "lat", "lon"), P(None, None, "lat", "lon"), P(None, "lat", "lon")),
        check_vma=False,
    )
```

profile of v0, /device:TPU:32, one launch (start us, length us, event | category | flops | bytes accessed | tf_op | source)
XLA Modules:
  0.0 176.5 jit_solution(2214828230962183955)
XLA Ops:
  7.2 0.0 all-reduce.7.cloned.1.call-start
  7.2 0.8 slice_bitcast_fusion
  8.1 0.8 fusion.13
  8.8 0.9 pad_subtract_fusion.1
  9.7 0.8 broadcast_maximum_fusion
  10.5 0.0 copy-start
  10.5 0.8 pad_maximum_fusion
  11.3 0.1 collective-permute-start
  11.4 1.7 collective-permute-start.1
  13.1 0.1 copy.56
  13.2 1.3 collective-permute-done
  14.5 0.1 copy.55
  14.6 0.0 collective-permute-done.1
  14.6 0.1 copy.57
  14.7 3.5 %collective-permute-start.2 = (f32[32,1,10]{0,1,2:T(1,128)S(1)}, f32[32,1,10]{0,1,2:T(1,128)S(1)}, u32[]{:S(2)}, u32[]{:S(2)}) collective-permute-start(f32[32,1,10]{0,1,2:T(1,128)S(1)} %get-tuple-element.34), channel_id=1, source_target_pairs={{0,32},{32,64},{64,96},{96,128},{128,160},{160,192},{192,224},{1,3... | collective-permute-start | bytes 3848 | tf_op jit(solution)/shard_map/ppermute | solution.py:14
  18.2 1.3 collective-permute-start.3
  19.5 0.0 collective-permute-done.2
  19.5 0.1 pad_maximum_fusion.7
  19.6 0.1 copy.72
  19.7 4.0 %collective-permute-done.3 = f32[32,1,10]{0,1,2:T(1,128)S(1)} collective-permute-done((f32[32,1,10]{0,1,2:T(1,128)S(1)}, f32[32,1,10]{0,1,2:T(1,128)S(1)}, u32[]{:S(2)}, u32[]{:S(2)}) %collective-permute-start.3) | collective-permute-done | bytes 1312 | tf_op jit(solution)/shard_map/ppermute | solution.py:15
  23.7 0.1 copy.70
  23.8 0.1 fusion.21
  24.0 0.9 subtract_add_fusion
  24.8 1.0 fusion.8
  25.8 0.8 fusion.12
  26.6 0.6 collective-permute-start.4
  27.2 1.2 collective-permute-start.5
  28.4 1.3 collective-permute-done.4
  29.8 0.0 collective-permute-done.5
  29.8 0.1 fusion.19
  29.9 4.2 %collective-permute-start.6 = (f32[16,1,10]{1,2,0:T(8,128)S(1)}, f32[16,1,10]{1,2,0:T(8,128)S(1)}, u32[]{:S(2)}, u32[]{:S(2)}) collective-permute-start(f32[16,1,10]{1,2,0:T(8,128)S(1)} %get-tuple-element.24), channel_id=1, source_target_pairs={{0,32},{32,64},{64,96},{96,128},{128,160},{160,192},{192,224},{1,3... | collective-permute-start | bytes 1928 | tf_op jit(solution)/shard_map/ppermute | solution.py:14
  34.1 1.3 collective-permute-start.7
  35.4 0.1 copy.65
  35.5 0.1 convert_element_type.21
  35.6 1.3 collective-permute-done.6
  37.0 4.7 %collective-permute-done.7 = f32[16,1,10]{1,2,0:T(8,128)S(1)} collective-permute-done((f32[16,1,10]{1,2,0:T(8,128)S(1)}, f32[16,1,10]{1,2,0:T(8,128)S(1)}, u32[]{:S(2)}, u32[]{:S(2)}) %collective-permute-start.7) | collective-permute-done | bytes 672 | tf_op jit(solution)/shard_map/ppermute | solution.py:15
  41.7 0.2 pad_maximum_fusion.2
  41.9 0.8 fusion.16
  42.6 0.1 copy.66
  42.7 0.1 convert_element_type.23
  42.9 46.2 %all_gather.3 = bf16[18,4096]{1,0:T(8,128)(2,1)S(1)} all-gather(bf16[18,128]{1,0:T(8,128)(2,1)S(1)} %pad_maximum_fusion.13), channel_id=1, replica_groups=mesh['lat'=8,'lon'=32] {'lon'}, dimensions={1}, use_global_device_ids=true | all-gather | bytes 152064 | tf_op jit(solution)/shard_map/all_gather | solution.py:51
  89.0 5.2 %fusion = f32[18,8,128]{2,0,1:T(8,128)} fusion(bf16[4096,8,128]{2,1,0:T(8,128)(2,1)} %param.9, bf16[18,4096]{1,0:T(8,128)(2,1)S(1)} %all_gather.3), kind=kOutput, calls=%fused_computation | convolution fusion | flops 150994944 | bytes 8609792 | tf_op jit(solution)/shard_map/rc,cam->ram/dot_general | solution.py:47
  94.2 0.0 all-reduce.7.cloned.1.call-update
  94.3 0.0 copy-done
  94.3 0.6 dynamic-slice
  94.9 71.0 %all-reduce.7.cloned.1.call-done = f32[18,8,128]{2,0,1:T(8,128)} async-done(((f32[18,8,128]{2,0,1:T(8,128)}), f32[18,8,128]{2,0,1:T(8,128)}) %all-reduce.7.cloned.1.call-update) | async-done | bytes 73744
  165.8 1.9 %constant_dynamic-slice_fusion.1 = f32[2,1,128]{2,0,1:T(2,128)} fusion(f32[18,8,128]{2,0,1:T(8,128)} %all-reduce.7.cloned.1.call-done, u32[]{:T(128)} %bitcast.10), kind=kLoop, calls=%fused_computation.56 | loop fusion | bytes 2052 | tf_op jit(solution)/shard_map/slice | solution.py:75
  167.7 1.9 %constant_dynamic-slice_fusion = f32[16,1,128]{2,0,1:T(8,128)} fusion(f32[18,8,128]{2,0,1:T(8,128)} %all-reduce.7.cloned.1.call-done, u32[]{:T(128)S(6)} %convert, u32[]{:T(128)} %bitcast.10), kind=kLoop, calls=%fused_computation.55 | loop fusion | bytes 16392 | tf_op jit(solution)/shard_map/slice | solution.py:76
  (9 shorter events, 0.1 us)
Async XLA Ops:
  7.2 158.7 %all-reduce.7.cloned.1.call-start = ((), (), s32[]{:S(2)}) async-start(), calls=%async_computation | async-start | bytes 196608
  10.5 83.8 %copy-start = (u32[256]{0:T(256)S(1)}, u32[256]{0:T(256)}, u32[]{:S(2)}) copy-start(u32[256]{0:T(256)} %constant.29) | copy-start | bytes 3076
  11.3 3.2 %collective-permute-start = (f32[32,16,1]{1,2,0:T(1,128)S(1)}, f32[32,16,1]{1,2,0:T(1,128)S(1)}, u32[]{:S(2)}, u32[]{:S(2)}) collective-permute-start(f32[32,16,1]{1,2,0:T(1,128)S(1)} %get-tuple-element.26), channel_id=1, source_target_pairs={{0,1},{1,2},{2,3},{3,4},{4,5},{5,6},{6,7},{7,8},{8,9},{9,10},{10,1... | collective-permute-start | bytes 6152 | tf_op jit(solution)/shard_map/ppermute | solution.py:14
  11.4 3.2 %collective-permute-start.1 = (f32[32,16,1]{1,2,0:T(1,128)S(1)}, f32[32,16,1]{1,2,0:T(1,128)S(1)}, u32[]{:S(2)}, u32[]{:S(2)}) collective-permute-start(f32[32,16,1]{1,2,0:T(1,128)S(1)} %get-tuple-element.27), channel_id=1, source_target_pairs={{1,0},{2,1},{3,2},{4,3},{5,4},{6,5},{7,6},{8,7},{9,8},{10,9},{11,1... | collective-permute-start | bytes 6152 | tf_op jit(solution)/shard_map/ppermute | solution.py:15
  14.7 4.8 %collective-permute-start.2 = (f32[32,1,10]{0,1,2:T(1,128)S(1)}, f32[32,1,10]{0,1,2:T(1,128)S(1)}, u32[]{:S(2)}, u32[]{:S(2)}) collective-permute-start(f32[32,1,10]{0,1,2:T(1,128)S(1)} %get-tuple-element.34), channel_id=1, source_target_pairs={{0,32},{32,64},{64,96},{96,128},{128,160},{160,192},{192,224},{1,3... | collective-permute-start | bytes 3848 | tf_op jit(solution)/shard_map/ppermute | solution.py:14
  18.2 5.5 %collective-permute-start.3 = (f32[32,1,10]{0,1,2:T(1,128)S(1)}, f32[32,1,10]{0,1,2:T(1,128)S(1)}, u32[]{:S(2)}, u32[]{:S(2)}) collective-permute-start(f32[32,1,10]{0,1,2:T(1,128)S(1)} %get-tuple-element.33), channel_id=1, source_target_pairs={{32,0},{64,32},{96,64},{128,96},{160,128},{192,160},{224,192},{33,... | collective-permute-start | bytes 3848 | tf_op jit(solution)/shard_map/ppermute | solution.py:15
  26.6 3.2 %collective-permute-start.4 = (f32[16,16,1]{1,2,0:T(1,128)S(1)}, f32[16,16,1]{1,2,0:T(1,128)S(1)}, u32[]{:S(2)}, u32[]{:S(2)}) collective-permute-start(f32[16,16,1]{1,2,0:T(1,128)S(1)} %get-tuple-element.35), channel_id=1, source_target_pairs={{0,1},{1,2},{2,3},{3,4},{4,5},{5,6},{6,7},{7,8},{8,9},{9,10},{10,1... | collective-permute-start | bytes 3080 | tf_op jit(solution)/shard_map/ppermute | solution.py:14
  27.2 2.6 %collective-permute-start.5 = (f32[16,16,1]{1,2,0:T(1,128)S(1)}, f32[16,16,1]{1,2,0:T(1,128)S(1)}, u32[]{:S(2)}, u32[]{:S(2)}) collective-permute-start(f32[16,16,1]{1,2,0:T(1,128)S(1)} %get-tuple-element.36), channel_id=1, source_target_pairs={{1,0},{2,1},{3,2},{4,3},{5,4},{6,5},{7,6},{8,7},{9,8},{10,9},{11,1... | collective-permute-start | bytes 3080 | tf_op jit(solution)/shard_map/ppermute | solution.py:15
  29.9 7.0 %collective-permute-start.6 = (f32[16,1,10]{1,2,0:T(8,128)S(1)}, f32[16,1,10]{1,2,0:T(8,128)S(1)}, u32[]{:S(2)}, u32[]{:S(2)}) collective-permute-start(f32[16,1,10]{1,2,0:T(8,128)S(1)} %get-tuple-element.24), channel_id=1, source_target_pairs={{0,32},{32,64},{64,96},{96,128},{128,160},{160,192},{192,224},{1,3... | collective-permute-start | bytes 1928 | tf_op jit(solution)/shard_map/ppermute | solution.py:14
  34.1 7.6 %collective-permute-start.7 = (f32[16,1,10]{1,2,0:T(8,128)S(1)}, f32[16,1,10]{1,2,0:T(8,128)S(1)}, u32[]{:S(2)}, u32[]{:S(2)}) collective-permute-start(f32[16,1,10]{1,2,0:T(8,128)S(1)} %get-tuple-element.25), channel_id=1, source_target_pairs={{32,0},{64,32},{96,64},{128,96},{160,128},{192,160},{224,192},{33,... | collective-permute-start | bytes 1928 | tf_op jit(solution)/shard_map/ppermute | solution.py:15
Sparse Core Ops, SparseCore 0:
  94.4 71.4 all-reduce.6
where the time goes:
time: 177 us
  waiting for transfers between devices  83.7 us (47%)
  blocking collectives  46.2 us (26%)
  between operations  14.2 us (8%)
  starting transfers between devices  13.9 us (8%)
  other arithmetic  6.9 us (4%)
  local copies, waits for them, and re-layouts  6.38 us (4%)
  matrix products  5.21 us (3%)
    unnamed x2, waiting for transfers between devices  71 us
    all_gather x1, blocking collectives, precondition(): total = row_adder(panel, lax.all_gather(vectors, 'lon', axis=1, tiled=True))  46.2 us
    ppermute x4, waiting for transfers between devices, extended(): after = lax.ppermute(initial, axis, down)  8.77 us
    ppermute x4, starting transfers between devices, extended(): before = lax.ppermute(last, axis, up)  8.36 us
    ppermute x4, starting transfers between devices, extended(): after = lax.ppermute(initial, axis, down)  5.53 us
    dot_general x1, matrix products, row_adder(): jnp.einsum('rc,cam->ram', piece, panel, preferred_element_type=jnp.float32)  5.21 us
    ppermute x4, waiting for transfers between devices, extended(): before = lax.ppermute(last, axis, up)  4 us
  transfers between devices with their start and end apart: 9, of which 6 were waited for; matrix products, arithmetic and copies ran while one was open for 1% of the time, Pallas kernels for 0%

commit v1 on v0

--- a/solution.py
+++ b/solution.py
@@ -48,7 +48,12 @@
 
 
 def precondition(vectors, panel):
-    total = row_adder(panel, lax.all_gather(vectors, "lon", axis=1, tiled=True))
+    total = row_adder(
+        panel,
+        jnp.concatenate(
+            lax.all_to_all(jnp.stack([vectors] * lax.axis_size("lon")), "lon", 0, 0), axis=1
+        ),
+    )
     return lax.psum_scatter(total, "lat", scatter_dimension=1, tiled=True)
 
 

time: 177 us -> 158 us (0.89)
  blocking collectives: 46.2 us -> 27.2 us
    all_gather x1 -> x0, blocking collectives: 46.2 us -> none  [precondition(): total = row_adder(panel, lax.all_gather(vectors, 'lon', axis=1, tiled=True))]
    all_to_all x0 -> x1, blocking collectives: none -> 27.2 us  [precondition(): lax.all_to_all(jnp.stack([vectors] * lax.axis_size('lon')), 'lon', 0, 0)]
where the time goes in v1:
time: 158 us; the launch traced here: 157 us
  waiting for transfers between devices  83.3 us (53%)
  blocking collectives  27.2 us (17%)
  between operations  14.2 us (9%)
  starting transfers between devices  13.9 us (9%)
  other arithmetic  6.88 us (4%)
  local copies, waits for them, and re-layouts  6.52 us (4%)
  matrix products  5.22 us (3%)
    unnamed x2, waiting for transfers between devices  70.5 us
    all_to_all x1, blocking collectives, precondition(): lax.all_to_all(jnp.stack([vectors] * lax.axis_size('lon')), 'lon', 0, 0)  27.2 us
    ppermute x4, waiting for transfers between devices, extended(): after = lax.ppermute(initial, axis, down)  8.77 us
    ppermute x4, starting transfers between devices, extended(): before = lax.ppermute(last, axis, up)  8.36 us
    ppermute x4, starting transfers between devices, extended(): after = lax.ppermute(initial, axis, down)  5.53 us
    dot_general x1, matrix products, row_adder(): jnp.einsum('rc,cam->ram', piece, panel, preferred_element_type=jnp.float32)  5.22 us
    ppermute x4, waiting for transfers between devices, extended(): before = lax.ppermute(last, axis, up)  4 us
  transfers between devices with their start and end apart: 9, of which 6 were waited for; matrix products, arithmetic and copies ran while one was open for 1% of the time, Pallas kernels for 0%

profile of v1, /device:TPU:32, one launch (start us, length us, event | category | flops | bytes accessed | tf_op | source)
XLA Modules:
  0.0 157.3 jit_solution(688284234761932759)
XLA Ops:
  7.2 0.0 all-reduce.7.cloned.1.call-start
  7.2 0.8 slice_bitcast_fusion
  8.1 0.8 fusion.12
  8.8 0.9 pad_subtract_fusion.1
  9.7 0.8 broadcast_maximum_fusion
  10.5 0.8 pad_maximum_fusion
  11.3 0.1 collective-permute-start
  11.3 1.7 %collective-permute-start.1 = (f32[32,16,1]{1,2,0:T(1,128)S(1)}, f32[32,16,1]{1,2,0:T(1,128)S(1)}, u32[]{:S(2)}, u32[]{:S(2)}) collective-permute-start(f32[32,16,1]{1,2,0:T(1,128)S(1)} %get-tuple-element.27), channel_id=1, source_target_pairs={{1,0},{2,1},{3,2},{4,3},{5,4},{6,5},{7,6},{8,7},{9,8},{10,9},{11,1... | collective-permute-start | bytes 6152 | tf_op jit(solution)/shard_map/ppermute | solution.py:15
  13.1 0.1 copy.56
  13.2 1.3 collective-permute-done
  14.5 0.1 copy.55
  14.6 0.0 collective-permute-done.1
  14.6 0.1 copy.57
  14.7 3.5 %collective-permute-start.2 = (f32[32,1,10]{0,1,2:T(1,128)S(1)}, f32[32,1,10]{0,1,2:T(1,128)S(1)}, u32[]{:S(2)}, u32[]{:S(2)}) collective-permute-start(f32[32,1,10]{0,1,2:T(1,128)S(1)} %get-tuple-element.34), channel_id=1, source_target_pairs={{0,32},{32,64},{64,96},{96,128},{128,160},{160,192},{192,224},{1,3... | collective-permute-start | bytes 3848 | tf_op jit(solution)/shard_map/ppermute | solution.py:14
  18.1 1.3 collective-permute-start.3
  19.4 0.0 collective-permute-done.2
  19.5 0.1 pad_maximum_fusion.7
  19.6 0.1 copy.73
  19.6 4.0 %collective-permute-done.3 = f32[32,1,10]{0,1,2:T(1,128)S(1)} collective-permute-done((f32[32,1,10]{0,1,2:T(1,128)S(1)}, f32[32,1,10]{0,1,2:T(1,128)S(1)}, u32[]{:S(2)}, u32[]{:S(2)}) %collective-permute-start.3) | collective-permute-done | bytes 1312 | tf_op jit(solution)/shard_map/ppermute | solution.py:15
  23.7 0.0 copy-start
  23.7 0.1 copy.71
  23.8 0.1 fusion.20
  24.0 0.9 subtract_add_fusion
  24.8 1.0 fusion.7
  25.8 0.8 fusion.11
  26.6 0.6 collective-permute-start.4
  27.2 1.2 collective-permute-start.5
  28.4 1.3 collective-permute-done.4
  29.8 0.0 collective-permute-done.5
  29.8 0.1 fusion.18
  29.9 4.2 %collective-permute-start.6 = (f32[16,1,10]{1,2,0:T(8,128)S(1)}, f32[16,1,10]{1,2,0:T(8,128)S(1)}, u32[]{:S(2)}, u32[]{:S(2)}) collective-permute-start(f32[16,1,10]{1,2,0:T(8,128)S(1)} %get-tuple-element.24), channel_id=1, source_target_pairs={{0,32},{32,64},{64,96},{96,128},{128,160},{160,192},{192,224},{1,3... | collective-permute-start | bytes 1928 | tf_op jit(solution)/shard_map/ppermute | solution.py:14
  34.1 1.3 collective-permute-start.7
  35.4 0.1 copy.65
  35.5 0.1 convert_element_type.21
  35.6 1.3 collective-permute-done.6
  37.0 4.7 %collective-permute-done.7 = f32[16,1,10]{1,2,0:T(8,128)S(1)} collective-permute-done((f32[16,1,10]{1,2,0:T(8,128)S(1)}, f32[16,1,10]{1,2,0:T(8,128)S(1)}, u32[]{:S(2)}, u32[]{:S(2)}) %collective-permute-start.7) | collective-permute-done | bytes 672 | tf_op jit(solution)/shard_map/ppermute | solution.py:15
  41.7 0.2 pad_maximum_fusion.2
  41.9 0.8 fusion.15
  42.6 0.1 copy.66
  42.7 0.1 convert_element_type.23
  42.9 27.2 %all_to_all.5 = bf16[32,18,128]{2,1,0:T(8,128)(2,1)S(1)} all-to-all(bf16[32,18,128]{2,1,0:T(8,128)(2,1)S(1)} %stack.2), channel_id=1, replica_groups=mesh['lat'=8,'lon'=32] {'lon'}, dimensions={0} | all-to-all | bytes 294912 | tf_op jit(solution)/shard_map/all_to_all | solution.py:54
  70.1 0.1 reshape.55
  70.2 5.2 %fusion = f32[18,8,128]{2,0,1:T(8,128)} fusion(bf16[18,4096,1]{1,0,2:T(8,128)(2,1)S(1)} %reshape.55, bf16[4096,8,128]{2,1,0:T(8,128)(2,1)} %param.9), kind=kOutput, calls=%fused_computation | convolution fusion | flops 150994944 | bytes 8609792 | tf_op jit(solution)/shard_map/rc,cam->ram/dot_general | solution.py:47
  75.5 0.0 all-reduce.7.cloned.1.call-update
  75.5 0.6 dynamic-slice
  76.1 70.5 %all-reduce.7.cloned.1.call-done = f32[18,8,128]{2,0,1:T(8,128)} async-done(((f32[18,8,128]{2,0,1:T(8,128)}), f32[18,8,128]{2,0,1:T(8,128)}) %all-reduce.7.cloned.1.call-update) | async-done | bytes 73744
  146.6 1.9 %constant_dynamic-slice_fusion.1 = f32[2,1,128]{2,0,1:T(2,128)} fusion(f32[18,8,128]{2,0,1:T(8,128)} %all-reduce.7.cloned.1.call-done, u32[]{:T(128)} %bitcast.10), kind=kLoop, calls=%fused_computation.55 | loop fusion | bytes 2052 | tf_op jit(solution)/shard_map/slice | solution.py:80
  148.5 1.9 %constant_dynamic-slice_fusion = f32[16,1,128]{2,0,1:T(8,128)} fusion(f32[18,8,128]{2,0,1:T(8,128)} %all-reduce.7.cloned.1.call-done, u32[]{:T(128)S(6)} %convert, u32[]{:T(128)} %bitcast.10), kind=kLoop, calls=%fused_computation.54 | loop fusion | bytes 16392 | tf_op jit(solution)/shard_map/slice | solution.py:81
  (12 shorter events, 0.2 us)
Async XLA Ops:
  7.2 139.4 %all-reduce.7.cloned.1.call-start = ((), (), s32[]{:S(2)}) async-start(), calls=%async_computation.1 | async-start | bytes 196608
  11.3 3.2 %collective-permute-start = (f32[32,16,1]{1,2,0:T(1,128)S(1)}, f32[32,16,1]{1,2,0:T(1,128)S(1)}, u32[]{:S(2)}, u32[]{:S(2)}) collective-permute-start(f32[32,16,1]{1,2,0:T(1,128)S(1)} %get-tuple-element.26), channel_id=1, source_target_pairs={{0,1},{1,2},{2,3},{3,4},{4,5},{5,6},{6,7},{7,8},{8,9},{9,10},{10,1... | collective-permute-start | bytes 6152 | tf_op jit(solution)/shard_map/ppermute | solution.py:14
  11.3 3.2 %collective-permute-start.1 = (f32[32,16,1]{1,2,0:T(1,128)S(1)}, f32[32,16,1]{1,2,0:T(1,128)S(1)}, u32[]{:S(2)}, u32[]{:S(2)}) collective-permute-start(f32[32,16,1]{1,2,0:T(1,128)S(1)} %get-tuple-element.27), channel_id=1, source_target_pairs={{1,0},{2,1},{3,2},{4,3},{5,4},{6,5},{7,6},{8,7},{9,8},{10,9},{11,1... | collective-permute-start | bytes 6152 | tf_op jit(solution)/shard_map/ppermute | solution.py:15
  14.7 4.8 %collective-permute-start.2 = (f32[32,1,10]{0,1,2:T(1,128)S(1)}, f32[32,1,10]{0,1,2:T(1,128)S(1)}, u32[]{:S(2)}, u32[]{:S(2)}) collective-permute-start(f32[32,1,10]{0,1,2:T(1,128)S(1)} %get-tuple-element.34), channel_id=1, source_target_pairs={{0,32},{32,64},{64,96},{96,128},{128,160},{160,192},{192,224},{1,3... | collective-permute-start | bytes 3848 | tf_op jit(solution)/shard_map/ppermute | solution.py:14
  18.1 5.5 %collective-permute-start.3 = (f32[32,1,10]{0,1,2:T(1,128)S(1)}, f32[32,1,10]{0,1,2:T(1,128)S(1)}, u32[]{:S(2)}, u32[]{:S(2)}) collective-permute-start(f32[32,1,10]{0,1,2:T(1,128)S(1)} %get-tuple-element.33), channel_id=1, source_target_pairs={{32,0},{64,32},{96,64},{128,96},{160,128},{192,160},{224,192},{33,... | collective-permute-start | bytes 3848 | tf_op jit(solution)/shard_map/ppermute | solution.py:15
  23.7 51.8 %copy-start = (u32[256]{0:T(256)S(1)}, u32[256]{0:T(256)}, u32[]{:S(2)}) copy-start(u32[256]{0:T(256)} %constant.29) | copy-start | bytes 3076
  26.6 3.2 %collective-permute-start.4 = (f32[16,16,1]{1,2,0:T(1,128)S(1)}, f32[16,16,1]{1,2,0:T(1,128)S(1)}, u32[]{:S(2)}, u32[]{:S(2)}) collective-permute-start(f32[16,16,1]{1,2,0:T(1,128)S(1)} %get-tuple-element.35), channel_id=1, source_target_pairs={{0,1},{1,2},{2,3},{3,4},{4,5},{5,6},{6,7},{7,8},{8,9},{9,10},{10,1... | collective-permute-start | bytes 3080 | tf_op jit(solution)/shard_map/ppermute | solution.py:14
  27.2 2.6 %collective-permute-start.5 = (f32[16,16,1]{1,2,0:T(1,128)S(1)}, f32[16,16,1]{1,2,0:T(1,128)S(1)}, u32[]{:S(2)}, u32[]{:S(2)}) collective-permute-start(f32[16,16,1]{1,2,0:T(1,128)S(1)} %get-tuple-element.36), channel_id=1, source_target_pairs={{1,0},{2,1},{3,2},{4,3},{5,4},{6,5},{7,6},{8,7},{9,8},{10,9},{11,1... | collective-permute-start | bytes 3080 | tf_op jit(solution)/shard_map/ppermute | solution.py:15
  29.9 7.0 %collective-permute-start.6 = (f32[16,1,10]{1,2,0:T(8,128)S(1)}, f32[16,1,10]{1,2,0:T(8,128)S(1)}, u32[]{:S(2)}, u32[]{:S(2)}) collective-permute-start(f32[16,1,10]{1,2,0:T(8,128)S(1)} %get-tuple-element.24), channel_id=1, source_target_pairs={{0,32},{32,64},{64,96},{96,128},{128,160},{160,192},{192,224},{1,3... | collective-permute-start | bytes 1928 | tf_op jit(solution)/shard_map/ppermute | solution.py:14
  34.1 7.6 %collective-permute-start.7 = (f32[16,1,10]{1,2,0:T(8,128)S(1)}, f32[16,1,10]{1,2,0:T(8,128)S(1)}, u32[]{:S(2)}, u32[]{:S(2)}) collective-permute-start(f32[16,1,10]{1,2,0:T(8,128)S(1)} %get-tuple-element.25), channel_id=1, source_target_pairs={{32,0},{64,32},{96,64},{128,96},{160,128},{192,160},{224,192},{33,... | collective-permute-start | bytes 1928 | tf_op jit(solution)/shard_map/ppermute | solution.py:15
Sparse Core Ops, SparseCore 0:
  75.6 70.9 all-reduce.6
